TPU v7x, 128 devices: a whole 4x4x4 slice. The times are simulated.
128 devices in a mesh: tm: 8 (over y, core), rows: 16 (over x, z).
Axes of the slice: x: 4, y: 4, z: 4, core: 2. Of those that a mesh axis runs over, the one named last changes fastest.
Arguments:
- latents: bfloat16 [16, 64, 128, 384], P('tm', 'rows'), may hold values from -6 to 6
- reward_weight: bfloat16 [16, 64, 128, 384], P('tm', 'rows'), may hold values from -6 to 6
- norm_gain: float32 [384], replicated, may hold values from 0.1 to 1.9
- conv_weight: bfloat16 [27, 384, 384], replicated, may hold values from -0.0625 to 0.0625
- scored_frames: int32 [8], replicated, may hold values from 0 to 15, as said below
Outputs:
- grad_latents: bfloat16 [16, 64, 128, 384], P('tm', 'rows')
- grad_weight: float32 [10368, 384], P(('tm', 'rows'))
- grad_gain: float32 [384], replicated
Inputs may be any that keep to these rules, and one draw needn't show every extreme that they name: `scored_frames`: distinct latent frame indices; the first frame 0 and the last frame 16 - 1 are always scored.
All inputs are finite; a program needn't handle non-finite values.
Results may differ from a plain program's by a relative error of at most 0.015.
Values may be sent and summed in bfloat16 or wider, within the bound.
A program may use at most 256 MiB of HBM per device.

v0:
```python
import jax
import jax.numpy as jnp
from jax import lax
from jax.sharding import PartitionSpec as P

EPSILON = 1e-06


def shifted(value, axis, steps):
    count = lax.axis_size(axis)
    initial, last = (max(0, -steps), min(count, count - steps))
    return lax.ppermute(value, axis, [(source, source + steps) for source in range(initial, last)])


def extended(cells, sides, width):
    for axis, dim in sides:
        count = lax.axis_size(axis)
        ends = count - 1
        head = lax.slice_in_dim(cells, 0, width, axis=dim)
        tail = lax.slice_in_dim(cells, cells.shape[dim] - width, cells.shape[dim], axis=dim)
        cells = jnp.concatenate(
            [
                lax.ppermute(tail, axis, [(i, (i + 1) % count) for i in range(ends)]),
                cells,
                lax.ppermute(head, axis, [((i + 1) % count, i) for i in range(ends)]),
            ],
            axis=dim,
        )
    return cells


def slope(value):
    sigmoid_v = jax.nn.sigmoid(value)
    return sigmoid_v * (1.0 + value * (1.0 - sigmoid_v))


def shards(latents, reward_weight, norm_gain, conv_weight, scored_frames):
    frames, height, columns, channels = latents.shape
    cell_count = frames * height * columns
    wide = latents.astype(jnp.float32)
    inverse = lax.rsqrt(jnp.mean(wide * wide, axis=-1, keepdims=True) + EPSILON)
    normed = wide * inverse
    activated = normed * norm_gain
    soft = jax.nn.silu(activated).astype(jnp.bfloat16)
    before = shifted(soft, "tm", 1)
    joined = jnp.concatenate([before, soft], axis=0)
    rimmed = extended(joined, (("rows", 1),), 1)
    soft_pad = jnp.pad(rimmed, ((0, 0), (0, 0), (1, 1), (0, 0)))
    conv_sum = jnp.zeros((cell_count, channels), jnp.float32)
    for offset in range(27):
        frame_off, row_off, col_off = (offset // 9, offset // 3 % 3, offset % 3)
        window = soft_pad[
            frame_off : frame_off + frames, row_off : row_off + height, col_off : col_off + columns
        ].reshape(cell_count, channels)
        conv_sum = conv_sum + jnp.dot(
            window, conv_weight[offset], preferred_element_type=jnp.float32
        )
    output = wide + conv_sum.reshape(wide.shape)
    frame_ids = lax.axis_index("tm") * frames + jnp.arange(frames, dtype=jnp.int32)
    scored_mask = jnp.any(frame_ids[:, None] == scored_frames[None, :], axis=1).astype(jnp.float32)
    grad_out = (
        scored_mask[:, None, None, None] * reward_weight.astype(jnp.float32) * slope(output)
    ).astype(jnp.bfloat16)
    grad_flat = grad_out.reshape(cell_count, channels)
    blocks = []
    for offset in range(27):
        frame_off, row_off, col_off = (offset // 9, offset // 3 % 3, offset % 3)
        source = soft_pad[
            frame_off : frame_off + frames, row_off : row_off + height, col_off : col_off + columns
        ].reshape(cell_count, channels)
        blocks.append(
            lax.dot_general(
                source, grad_flat, (((0,), (0,)), ((), ())), preferred_element_type=jnp.float32
            )
        )
    weight_local = jnp.concatenate(blocks, axis=0)
    following = shifted(grad_out, "tm", -1)
    grad_join = jnp.concatenate([grad_out, following], axis=0)
    grad_rim = extended(grad_join, (("rows", 1),), 1)
    grad_pad = jnp.pad(grad_rim, ((0, 0), (0, 0), (1, 1), (0, 0)))
    grad_sum = jnp.zeros((cell_count, channels), jnp.float32)
    for offset in range(27):
        frame_off, row_off, col_off = (offset // 9, offset // 3 % 3, offset % 3)
        window = grad_pad[
            2 - frame_off : 2 - frame_off + frames,
            2 - row_off : 2 - row_off + height,
            2 - col_off : 2 - col_off + columns,
        ].reshape(cell_count, channels)
        grad_sum = grad_sum + lax.dot_general(
            window,
            conv_weight[offset],
            (((1,), (1,)), ((), ())),
            preferred_element_type=jnp.float32,
        )
    grad_soft = grad_sum.reshape(wide.shape)
    weight_shard = lax.psum_scatter(weight_local, ("tm", "rows"), scatter_dimension=0, tiled=True)
    grad_act = grad_soft * slope(activated)
    grad_gain = lax.psum(jnp.sum(grad_act * normed, axis=(0, 1, 2)), ("tm", "rows"))
    scaled = grad_act * norm_gain
    grad_latents = (
        grad_out.astype(jnp.float32)
        + inverse * (scaled - normed * jnp.mean(scaled * normed, axis=-1, keepdims=True))
    ).astype(jnp.bfloat16)
    return (grad_latents, weight_shard, grad_gain)


def solution(mesh):
    placed = (P("tm", "rows", None, None), P("tm", "rows", None, None), P(), P(), P())
    return jax.shard_map(
        shards,
        mesh=mesh,
        in_specs=placed,
        out_specs=(P("tm", "rows", None, None), P(("tm", "rows"), None), P()),
        check_vma=False,
    )
```

profile of v0, /device:TPU:0, one launch (start us, length us, event | category | flops | bytes accessed | tf_op | source)
XLA Modules:
  0.0 951.6 jit_solution(14179790623873040840)
XLA Ops:
  7.9 3.0 fusion.78
  11.9 4.4 collective-permute-start.1
  21.3 3.0 fusion.114
  32.2 3.0 fusion.102
  37.6 3.0 fusion.126
  42.9 3.0 fusion.138
  48.3 3.0 fusion.162
  53.6 3.0 fusion.66
  57.7 3.0 fusion.90
  60.8 3.7 select_maximum_fusion.3
  64.5 6.3 fusion.243
  73.1 3.0 fusion.106
  78.5 3.0 fusion.110
  83.8 3.0 fusion.118
  89.1 3.0 fusion.122
  94.4 3.0 fusion.130
  105.0 3.1 fusion.142
  110.3 3.0 fusion.146
  115.6 3.0 fusion.154
  120.9 3.0 fusion.158
  126.1 3.0 fusion.166
  131.4 3.0 fusion.70
  136.7 3.0 fusion.74
  142.0 3.3 fusion.82
  147.6 3.0 fusion.86
  152.9 3.0 fusion.94
  158.2 3.0 fusion.98
  162.4 16.3 %add_add_fusion.1 = f32[1024,384]{1,0:T(8,128)} fusion(f32[1024,384]{1,0:T(8,128)} %fusion.66, f32[1024,384]{1,0:T(8,128)} %fusion.70, f32[1024,384]{1,0:T(8,128)} %fusion.74, f32[1024,384]{1,0:T(8,128)} %fusion.78, f32[1024,384]{1,0:T(8,128)} %fusion.82, f32[1024,384]{1,0:T(8,128)} %fusion.86, f32[1024,384]{1,0:T(8,128)} %fusion.90, ...), kind=kOutput, calls=%fused_computation.45 | convolution fusion | flops 312213504 | bytes 43548672 | tf_op jit(solution)/shard_map/dot_general | solution.py:55
  178.7 3.1 copy.241
  224.6 393.1 %fusion = f32[96,384]{1,0:T(8,128)S(1)} fusion(f32[10368,384]{1,0:T(8,128)} %fusion.42), kind=kCustom, calls=%all-reduce-scatter | all-reduce-scatter fusion | flops 4718593 | bytes 16072704
  624.3 4.7 collective-permute-done.25
  631.7 9.2 collective-permute-start.16
  646.2 4.0 collective-permute-start.19
  652.5 8.2 collective-permute-start.21
  660.7 3.7 collective-permute-start.22
  664.4 3.5 collective-permute-start.23
  673.7 3.4 collective-permute-start.7
  677.1 5.8 collective-permute-start.8
  682.8 4.5 collective-permute-start.9
  691.5 32.3 %concatenate.44 = f32[2001,384]{1,0:T(8,128)} concatenate(f32[81,384]{1,0:T(8,128)} %copy-done.18, f32[96,384]{1,0:T(8,128)} %collective-permute-done.24, f32[96,384]{1,0:T(8,128)} %collective-permute-done.23, f32[96,384]{1,0:T(8,128)} %collective-permute-done.22, f32[96,384]{1,0:T(8,128)} %collective-permute-done.21, f32[96,384]{1,0:T(8,128)} %copy-done.14, ...), dimensions={0} | concatenate | bytes 6147072
  736.0 4.3 collective-permute-done.5
  740.3 4.7 select_maximum_fusion
  745.0 6.2 fusion.242
  753.5 3.0 fusion.104
  758.8 3.1 fusion.108
  764.1 3.0 fusion.116
  769.4 3.1 fusion.120
  774.8 3.0 fusion.128
  780.1 3.0 fusion.132
  785.4 3.0 fusion.140
  790.7 3.0 fusion.144
  796.0 3.0 fusion.152
  801.3 3.0 fusion.156
  806.7 3.0 fusion.164
  812.1 3.1 fusion.68
  817.5 3.0 fusion.72
  822.8 3.0 fusion.80
  828.1 3.1 fusion.84
  833.7 3.0 fusion.92
  837.9 3.0 fusion.96
  847.4 3.0 fusion.100
  857.3 3.0 fusion.136
  868.7 13.0 %add_add_fusion = f32[1024,384]{1,0:T(8,128)S(1)} fusion(f32[1024,384]{1,0:T(8,128)} %fusion.64, f32[1024,384]{1,0:T(8,128)} %fusion.68, f32[1024,384]{1,0:T(8,128)} %fusion.72, f32[1024,384]{1,0:T(8,128)S(1)} %copy-done.3, f32[1024,384]{1,0:T(8,128)} %fusion.80, f32[1024,384]{1,0:T(8,128)} %fusion.84, f32[1024,384]{1,0:T(8,128)S(1)} %fusion.88, ...), kind=kOutput, calls=%fused_computation.43 | convolution fusion | flops 312213504 | bytes 43548672 | tf_op jit(solution)/shard_map/dot_general | solution.py:89
  887.6 63.9 %psum.7 = f32[384]{0:T(512)} all-reduce(f32[384]{0:T(512)S(1)} %get-tuple-element.15), channel_id=1, replica_groups=mesh['tm'=8,'rows'=16] {'tm','rows'}, use_global_device_ids=true, to_apply=%region_5.6 | all-reduce | flops 384 | bytes 3072 | tf_op jit(solution)/shard_map/psum | solution.py:98
  (203 shorter events, 222.2 us)
Async XLA Ops:
  0.6 1.7 copy-start.19
  2.2 16.9 %copy-start.1 = (bf16[2,4,128,384]{2,3,1,0:T(8,128)(2,1)}, bf16[2,4,128,384]{2,3,1,0:T(8,128)(2,1)S(1)}, u32[]{:S(2)}) copy-start(bf16[2,4,128,384]{2,3,1,0:T(8,128)(2,1)S(1)} %copy.213) | copy-start | bytes 2359300
  2.9 4.8 copy-start.20
  2.9 8.0 collective-permute-start
  11.9 15.5 %collective-permute-start.1 = (bf16[4,1,128,384]{2,3,1,0:T(8,128)(2,1)}, bf16[4,1,128,384]{2,3,1,0:T(8,128)(2,1)S(1)}, u32[]{:S(2)}, u32[]{:S(2)}) collective-permute-start(bf16[4,1,128,384]{2,3,1,0:T(8,128)(2,1)} %get-tuple-element.72), channel_id=1, source_target_pairs={{0,1},{1,2},{2,3},{3,4},{4,5},{5,6},{6,7},{7,8},{8,9},{9,10},{10,1... | collective-permute-start | bytes 1179656 | tf_op jit(solution)/shard_map/ppermute | solution.py:23
  16.3 11.1 %collective-permute-start.2 = (bf16[4,1,128,384]{2,3,1,0:T(8,128)(2,1)}, bf16[4,1,128,384]{2,3,1,0:T(8,128)(2,1)S(1)}, u32[]{:S(2)}, u32[]{:S(2)}) collective-permute-start(bf16[4,1,128,384]{2,3,1,0:T(8,128)(2,1)} %get-tuple-element.73), channel_id=1, source_target_pairs={{1,0},{2,1},{3,2},{4,3},{5,4},{6,5},{7,6},{8,7},{9,8},{10,9},{11,1... | collective-permute-start | bytes 1179656 | tf_op jit(solution)/shard_map/ppermute | solution.py:25
  27.4 33.4 %copy-start.8 = (bf16[4,1,128,384]{2,3,1,0:T(8,128)(2,1)}, bf16[4,1,128,384]{2,3,1,0:T(8,128)(2,1)S(1)}, u32[]{:S(2)}) copy-start(bf16[4,1,128,384]{2,3,1,0:T(8,128)(2,1)S(1)} %collective-permute-done.1) | copy-start | bytes 1179652
  64.5 6.4 copy-start
  178.7 9.9 %slice-start = ((s8[4718592]{0:T(1024)(128)(4,1)}), s8[524288]{0:T(1024)(128)(4,1)S(1)}, s32[]{:S(2)}) async-start(s8[4718592]{0:T(1024)(128)(4,1)} %bitcast.436), calls=%async_computation | async-start | bytes 1048576
  181.8 6.8 slice-start.1
  184.5 2.6 copy-start.9
  617.8 12.6 %collective-permute-start.10 = (f32[96,384]{1,0:T(8,128)S(1)}, f32[96,384]{1,0:T(8,128)S(1)}, u32[]{:S(2)}, u32[]{:S(2)}) collective-permute-start(f32[96,384]{1,0:T(8,128)S(1)} %fusion), channel_id=1, source_target_pairs={{0,5},{1,6},{2,7},{3,8},{4,9},{5,10},{6,11},{7,12},{8,13},{9,14},{... | collective-permute-start | bytes 442376
  619.1 12.6 %collective-permute-start.11 = (f32[96,384]{1,0:T(8,128)S(1)}, f32[96,384]{1,0:T(8,128)S(1)}, u32[]{:S(2)}, u32[]{:S(2)}) collective-permute-start(f32[96,384]{1,0:T(8,128)S(1)} %fusion), channel_id=1, source_target_pairs={{0,6},{1,7},{2,8},{3,9},{4,10},{5,11},{6,12},{7,13},{8,14},{9,15},... | collective-permute-start | bytes 442376
  620.4 8.7 collective-permute-start.25
  621.7 19.2 %collective-permute-start.12 = (f32[96,384]{1,0:T(8,128)S(1)}, f32[96,384]{1,0:T(8,128)S(1)}, u32[]{:S(2)}, u32[]{:S(2)}) collective-permute-start(f32[96,384]{1,0:T(8,128)S(1)} %fusion), channel_id=1, source_target_pairs={{0,7},{1,8},{2,9},{3,10},{4,11},{5,12},{6,13},{7,14},{8,15},{9,16}... | collective-permute-start | bytes 442376
  623.0 19.2 %collective-permute-start.13 = (f32[96,384]{1,0:T(8,128)S(1)}, f32[96,384]{1,0:T(8,128)S(1)}, u32[]{:S(2)}, u32[]{:S(2)}) collective-permute-start(f32[96,384]{1,0:T(8,128)S(1)} %fusion), channel_id=1, source_target_pairs={{0,8},{1,9},{2,10},{3,11},{4,12},{5,13},{6,14},{7,15},{8,16},{9,17... | collective-permute-start | bytes 442376
  629.0 38.8 %copy-start.18 = (f32[81,384]{1,0:T(8,128)}, f32[81,384]{1,0:T(8,128)S(1)}, u32[]{:S(2)}) copy-start(f32[81,384]{1,0:T(8,128)S(1)} %collective-permute-done.25) | copy-start | bytes 373252
  629.1 14.5 %collective-permute-start.14 = (f32[96,384]{1,0:T(8,128)S(1)}, f32[96,384]{1,0:T(8,128)S(1)}, u32[]{:S(2)}, u32[]{:S(2)}) collective-permute-start(f32[96,384]{1,0:T(8,128)S(1)} %fusion), channel_id=1, source_target_pairs={{0,9},{1,10},{2,11},{3,12},{4,13},{5,14},{6,15},{7,16},{8,17},{9,1... | collective-permute-start | bytes 442376
  630.4 15.8 %collective-permute-start.15 = (f32[96,384]{1,0:T(8,128)S(1)}, f32[96,384]{1,0:T(8,128)S(1)}, u32[]{:S(2)}, u32[]{:S(2)}) collective-permute-start(f32[96,384]{1,0:T(8,128)S(1)} %fusion), channel_id=1, source_target_pairs={{0,10},{1,11},{2,12},{3,13},{4,14},{5,15},{6,16},{7,17},{8,18},{9,... | collective-permute-start | bytes 442376
  631.7 18.5 %collective-permute-start.16 = (f32[96,384]{1,0:T(8,128)S(1)}, f32[96,384]{1,0:T(8,128)S(1)}, u32[]{:S(2)}, u32[]{:S(2)}) collective-permute-start(f32[96,384]{1,0:T(8,128)S(1)} %fusion), channel_id=1, source_target_pairs={{0,11},{1,12},{2,13},{3,14},{4,15},{5,16},{6,17},{7,18},{8,19},{9,... | collective-permute-start | bytes 442376
  640.9 84.5 %collective-permute-start.3 = (bf16[2,4,128,384]{2,3,1,0:T(8,128)(2,1)S(1)}, bf16[2,4,128,384]{2,3,1,0:T(8,128)(2,1)S(1)}, u32[]{:S(2)}, u32[]{:S(2)}) collective-permute-start(bf16[2,4,128,384]{2,3,1,0:T(8,128)(2,1)S(1)} %multiply_convert_fusion), channel_id=1, source_target_pairs={{16,0},{32,16},{48,32},{64,48},{80,64},{96,80},{112,96},{17,1},{33... | collective-permute-start | bytes 2359304 | tf_op jit(solution)/shard_map/ppermute | solution.py:12
  642.2 10.2 %collective-permute-start.17 = (f32[96,384]{1,0:T(8,128)S(1)}, f32[96,384]{1,0:T(8,128)S(1)}, u32[]{:S(2)}, u32[]{:S(2)}) collective-permute-start(f32[96,384]{1,0:T(8,128)S(1)} %fusion), channel_id=1, source_target_pairs={{0,12},{1,13},{2,14},{3,15},{4,16},{5,17},{6,18},{7,19},{8,20},{9,... | collective-permute-start | bytes 442376
  643.5 17.1 %collective-permute-start.18 = (f32[96,384]{1,0:T(8,128)S(1)}, f32[96,384]{1,0:T(8,128)S(1)}, u32[]{:S(2)}, u32[]{:S(2)}) collective-permute-start(f32[96,384]{1,0:T(8,128)S(1)} %fusion), channel_id=1, source_target_pairs={{0,13},{1,14},{2,15},{3,16},{4,17},{5,18},{6,19},{7,20},{8,21},{9,... | collective-permute-start | bytes 442376
  646.2 18.2 %collective-permute-start.19 = (f32[96,384]{1,0:T(8,128)S(1)}, f32[96,384]{1,0:T(8,128)S(1)}, u32[]{:S(2)}, u32[]{:S(2)}) collective-permute-start(f32[96,384]{1,0:T(8,128)S(1)} %fusion), channel_id=1, source_target_pairs={{0,14},{1,15},{2,16},{3,17},{4,18},{5,19},{6,20},{7,21},{8,22},{9,... | collective-permute-start | bytes 442376
  650.2 17.6 %collective-permute-start.20 = (f32[96,384]{1,0:T(8,128)S(1)}, f32[96,384]{1,0:T(8,128)S(1)}, u32[]{:S(2)}, u32[]{:S(2)}) collective-permute-start(f32[96,384]{1,0:T(8,128)S(1)} %fusion), channel_id=1, source_target_pairs={{0,15},{1,16},{2,17},{3,18},{4,19},{5,20},{6,21},{7,22},{8,23},{9,... | collective-permute-start | bytes 442376
  652.4 18.3 %copy-start.11 = (f32[96,384]{1,0:T(8,128)}, f32[96,384]{1,0:T(8,128)S(1)}, u32[]{:S(2)}) copy-start(f32[96,384]{1,0:T(8,128)S(1)} %collective-permute-done.17) | copy-start | bytes 442372
  652.5 18.7 %collective-permute-start.21 = (f32[96,384]{1,0:T(8,128)S(1)}, f32[96,384]{1,0:T(8,128)}, u32[]{:S(2)}, u32[]{:S(2)}) collective-permute-start(f32[96,384]{1,0:T(8,128)S(1)} %fusion), channel_id=1, source_target_pairs={{0,16},{1,17},{2,18},{3,19},{4,20},{5,21},{6,22},{7,23},{8,24},{9,... | collective-permute-start | bytes 442376
  660.7 10.1 %copy-start.12 = (f32[96,384]{1,0:T(8,128)}, f32[96,384]{1,0:T(8,128)S(1)}, u32[]{:S(2)}) copy-start(f32[96,384]{1,0:T(8,128)S(1)} %collective-permute-done.18) | copy-start | bytes 442372
  660.7 13.0 %collective-permute-start.22 = (f32[96,384]{1,0:T(8,128)S(1)}, f32[96,384]{1,0:T(8,128)}, u32[]{:S(2)}, u32[]{:S(2)}) collective-permute-start(f32[96,384]{1,0:T(8,128)S(1)} %fusion), channel_id=1, source_target_pairs={{0,17},{1,18},{2,19},{3,20},{4,21},{5,22},{6,23},{7,24},{8,25},{9,... | collective-permute-start | bytes 442376
  664.4 6.4 copy-start.13
  664.4 12.6 %collective-permute-start.23 = (f32[96,384]{1,0:T(8,128)S(1)}, f32[96,384]{1,0:T(8,128)}, u32[]{:S(2)}, u32[]{:S(2)}) collective-permute-start(f32[96,384]{1,0:T(8,128)S(1)} %fusion), channel_id=1, source_target_pairs={{0,18},{1,19},{2,20},{3,21},{4,22},{5,23},{6,24},{7,25},{8,26},{9,... | collective-permute-start | bytes 442376
  667.9 2.9 copy-start.14
  667.9 15.0 %collective-permute-start.24 = (f32[96,384]{1,0:T(8,128)S(1)}, f32[96,384]{1,0:T(8,128)}, u32[]{:S(2)}, u32[]{:S(2)}) collective-permute-start(f32[96,384]{1,0:T(8,128)S(1)} %fusion), channel_id=1, source_target_pairs={{0,19},{1,20},{2,21},{3,22},{4,23},{5,24},{6,25},{7,26},{8,27},{9,... | collective-permute-start | bytes 442376
  671.2 19.0 %collective-permute-start.6 = (f32[96,384]{1,0:T(8,128)S(1)}, f32[96,384]{1,0:T(8,128)S(1)}, u32[]{:S(2)}, u32[]{:S(2)}) collective-permute-start(f32[96,384]{1,0:T(8,128)S(1)} %fusion), channel_id=1, source_target_pairs={{0,1},{1,2},{2,3},{3,4},{4,5},{5,6},{6,7},{7,8},{8,9},{9,10},{10,1... | collective-permute-start | bytes 442376
  673.7 16.4 %collective-permute-start.7 = (f32[96,384]{1,0:T(8,128)S(1)}, f32[96,384]{1,0:T(8,128)S(1)}, u32[]{:S(2)}, u32[]{:S(2)}) collective-permute-start(f32[96,384]{1,0:T(8,128)S(1)} %fusion), channel_id=1, source_target_pairs={{0,2},{1,3},{2,4},{3,5},{4,6},{5,7},{6,8},{7,9},{8,10},{9,11},{10,... | collective-permute-start | bytes 442376
  677.1 13.1 %collective-permute-start.8 = (f32[96,384]{1,0:T(8,128)S(1)}, f32[96,384]{1,0:T(8,128)S(1)}, u32[]{:S(2)}, u32[]{:S(2)}) collective-permute-start(f32[96,384]{1,0:T(8,128)S(1)} %fusion), channel_id=1, source_target_pairs={{0,3},{1,4},{2,5},{3,6},{4,7},{5,8},{6,9},{7,10},{8,11},{9,12},{10... | collective-permute-start | bytes 442376
  682.8 8.6 collective-permute-start.9
  690.1 0.7 copy-start.15
  690.1 0.7 copy-start.16
  690.8 0.7 copy-start.17
  726.8 9.2 collective-permute-start.4
  728.1 12.1 %collective-permute-start.5 = (bf16[4,1,128,384]{2,3,1,0:T(8,128)(2,1)}, bf16[4,1,128,384]{2,3,1,0:T(8,128)(2,1)}, u32[]{:S(2)}, u32[]{:S(2)}) collective-permute-start(bf16[4,1,128,384]{2,3,1,0:T(8,128)(2,1)} %get-tuple-element.68), channel_id=1, source_target_pairs={{1,0},{2,1},{3,2},{4,3},{5,4},{6,5},{7,6},{8,7},{9,8},{10,9},{11,1... | collective-permute-start | bytes 1179656 | tf_op jit(solution)/shard_map/ppermute | solution.py:25
  736.0 9.0 copy-start.10
  851.8 4.3 copy-start.5
  856.1 4.2 copy-start.6
  863.4 3.1 copy-start.4
  866.9 1.8 copy-start.3
  866.9 1.8 copy-start.7
  881.8 1.7 copy-start.2
where the time goes:
time: 960 us; the launch traced here: 952 us
  blocking collectives  457 us (48%)
  matrix products  223 us (23%)
  local copies, waits for them, and re-layouts  166 us (17%)
  starting transfers between devices  74.3 us (8%)
  other arithmetic  20 us (2%)
  waiting for transfers between devices  9.67 us (1%)
    unnamed x1, blocking collectives  393 us
    dot_general x27, matrix products, shards(): jnp.dot(window, conv_weight[offset], preferred_element_type=jnp.float32)  94.2 us
    dot_general x27, matrix products, shards(): lax.dot_general(window, conv_weight[offset], (((1,), (1,)), ((), ())), pr...  88.7 us
    psum x1, blocking collectives, shards(): lax.psum(jnp.sum(grad_act * normed, axis=(0, 1, 2)), ('tm', 'rows'))  63.9 us
    slice x27, local copies, waits for them, and re-layouts, shards(): soft_pad[frame_off:frame_off + frames, row_off:row_off + height, col_off:...  63.8 us
    unnamed x20, starting transfers between devices  62.9 us
    slice x28, local copies, waits for them, and re-layouts, shards(): grad_pad[2 - frame_off:2 - frame_off + frames, 2 - row_off:2 - row_off +...  55.2 us
    unnamed x52, local copies, waits for them, and re-layouts  40.3 us
  transfers between devices with their start and end apart: 26, of which 3 were waited for; matrix products, arithmetic and copies ran while one was open for 6% of the time, Pallas kernels for 0%

commit v1 on v0

v1 whole, which is shorter than its diff:
```python
import functools

import jax
import jax.numpy as jnp
from jax import lax
from jax.experimental import pallas as pl
from jax.experimental.pallas import tpu as pltpu
from jax.sharding import PartitionSpec as P

MESH = pl.DeviceIdType.MESH
EPSILON = 1e-06
BF = jnp.bfloat16
F32 = jnp.float32
FR, HT, WD, CH = 2, 4, 128, 384
FLAT = HT * WD
OWN = 81
PAD = 96
TAPROWS = 27 * CH
ORDERS = ((0, 1, 2), (1, 2, 0), (2, 0, 1))


def sigmoid(value):
    return 0.5 + 0.5 * jnp.tanh(0.5 * value)


def slope(value):
    s = sigmoid(value)
    return s * (1.0 + value * (1.0 - s))


def normalise(cells):
    wide = cells.astype(F32)
    inverse = lax.rsqrt(jnp.mean(wide * wide, axis=-1, keepdims=True) + EPSILON)
    return wide, inverse, wide * inverse


def down(x):
    row = lax.broadcasted_iota(jnp.int32, x.shape, 0)
    return jnp.where(row == 0, 0.0, pltpu.roll(x, 1, 0))


def up(x):
    row = lax.broadcasted_iota(jnp.int32, x.shape, 0)
    return jnp.where(row == x.shape[0] - 1, 0.0, pltpu.roll(x, x.shape[0] - 1, 0))


def kernel(
    lat, rew, gain, wgt_hbm, scored,
    out_lat, out_w, out_gain,
    wgt, ext, extt, gout, gsh, prod, gw,
    cs, cr, r1, r2, r3, r4,
    gacc, gt, gx, gz, gmid,
    wsem, hs, hr, ks, kr, css, crs, ss, rs, gss, grs,
):
    tm = lax.axis_index("tm")
    row = lax.axis_index("rows")
    core = tm % 2
    place = (tm // 2, row // 4, row % 4)

    def device(coords, c):
        return {"tm": coords[0] * 2 + c, "rows": coords[1] * 4 + coords[2]}

    def flip(v):
        return v + 1 - 2 * (v % 2)

    other = []
    for v in place:
        second = core * flip(v) + (1 - core) * (3 - v)
        first = core * (3 - v) + (1 - core) * flip(v)
        other.append((v, second, first, (v + 2) % 4))

    def peer(axis, q):
        coords = list(place)
        coords[axis] = other[axis][q]
        return device(coords, core)

    def pick(axis, q):
        if isinstance(q, int):
            return other[axis][q]
        o = other[axis]
        return jnp.where(q == 0, o[0], jnp.where(q == 1, o[1], jnp.where(q == 2, o[2], o[3])))

    tm_next, tm_prev = (tm + 1) % 8, (tm + 7) % 8
    row_next, row_prev = (row + 1) % 16, (row + 15) % 16
    twin = {"tm": tm + 1 - 2 * core, "rows": row}

    barrier = pltpu.get_barrier_semaphore()
    greeted = 0
    for dt, dr in ((1, 0), (7, 0), (0, 1), (0, 15), (1, 1), (1, 15), (7, 1), (7, 15)):
        pl.semaphore_signal(
            barrier, 1, device_id={"tm": (tm + dt) % 8, "rows": (row + dr) % 16}, device_id_type=MESH
        )
        greeted += 1
    for dt in range(2, 7):
        pl.semaphore_signal(barrier, 1, device_id={"tm": (tm + dt) % 8, "rows": row}, device_id_type=MESH)
        greeted += 1
    for axis in (1, 2):
        for q in (1, 2, 3):
            pl.semaphore_signal(barrier, 1, device_id=peer(axis, q), device_id_type=MESH)
            greeted += 1

    load = pltpu.make_async_copy(wgt_hbm, wgt, wsem)
    load.start()

    g_row = gain[...]

    def soften(cells, keep=None):
        _, _, normed = normalise(cells)
        act = normed * g_row
        value = act * sigmoid(act)
        if keep is not None:
            value = value * keep
        return value.astype(BF)

    def own_soft(i, _):
        f, r = i // HT, i % HT
        ext[2 + f, 1 + r] = soften(lat[f, r])
        return 0

    lax.fori_loop(0, FR * HT, own_soft, 0)

    pl.semaphore_wait(barrier, greeted)

    def send(src, dst, a, b, target):
        copy = pltpu.make_async_remote_copy(
            src_ref=src, dst_ref=dst, send_sem=a, recv_sem=b, device_id=target, device_id_type=MESH
        )
        copy.start()
        return copy

    def halo(copies, sems, src, dst, i, dt, dr):
        copies.append(
            send(src, dst, sems[0].at[i], sems[1].at[i], {"tm": (tm + dt) % 8, "rows": (row + dr) % 16})
        )

    copies = []
    pair = pl.ds(0, 2)
    halo(copies, (hs, hr), lat, ext.at[pair, pl.ds(1, HT)], 0, 1, 0)
    halo(copies, (hs, hr), lat.at[pair, HT - 1], ext.at[pl.ds(2, 2), 0], 1, 0, 1)
    halo(copies, (hs, hr), lat.at[pair, 0], ext.at[pl.ds(2, 2), HT + 1], 2, 0, 15)
    halo(copies, (hs, hr), lat.at[pair, HT - 1], ext.at[pair, 0], 3, 1, 1)
    halo(copies, (hs, hr), lat.at[pair, 0], ext.at[pair, HT + 1], 4, 1, 15)
    for copy in copies:
        copy.wait_recv()

    has_prev = jnp.where(tm > 0, 1.0, 0.0).astype(F32)
    has_top = jnp.where(row > 0, 1.0, 0.0).astype(F32)
    has_bot = jnp.where(row < 15, 1.0, 0.0).astype(F32)

    def halo_mid(i, _):
        f, r = i // HT, 1 + i % HT
        ext[f, r] = soften(ext[f, r], has_prev)
        return 0

    lax.fori_loop(0, FR * HT, halo_mid, 0)

    def halo_edge(f, _):
        keep = jnp.where(f < 2, has_prev, 1.0)
        ext[f, 0] = soften(ext[f, 0], keep * has_top)
        ext[f, HT + 1] = soften(ext[f, HT + 1], keep * has_bot)
        return 0

    lax.fori_loop(0, 4, halo_edge, 0)

    load.wait()

    def forward(f, _):
        left = jnp.concatenate(
            [ext[f + t // 3, pl.ds(t % 3, HT)].reshape(FLAT, CH) for t in range(9)], axis=1
        )
        right = jnp.concatenate(
            [jnp.concatenate([wgt[3 * t + c] for c in range(3)], axis=1) for t in range(9)], axis=0
        )
        prod[...] = jnp.dot(left, right, preferred_element_type=F32)
        frame = tm * FR + f
        mask = jnp.float32(0.0)
        for i in range(8):
            mask = jnp.maximum(mask, jnp.where(scored[i] == frame, 1.0, 0.0))

        def one_row(r, _):
            at = pl.ds(pl.multiple_of(r * WD, WD), WD)
            conv = down(prod[at, 0:CH]) + prod[at, CH : 2 * CH] + up(prod[at, 2 * CH : 3 * CH])
            value = lat[f, r].astype(F32) + conv
            grad = mask * rew[f, r].astype(F32) * slope(value)
            low = grad.astype(BF)
            wide = low.astype(F32)
            gout[f, 1 + r] = low
            to = pl.ds(pl.multiple_of(f * FLAT + r * WD, WD), WD)
            gsh[to, 0:CH] = up(wide).astype(BF)
            gsh[to, CH : 2 * CH] = low
            gsh[to, 2 * CH : 3 * CH] = down(wide).astype(BF)
            return 0

        lax.fori_loop(0, HT, one_row, 0)
        return 0

    lax.fori_loop(0, FR, forward, 0)

    gcopies = []
    halo(gcopies, (ks, kr), gout.at[pair, pl.ds(1, HT)], gout.at[pl.ds(2, 2), pl.ds(1, HT)], 0, 7, 0)
    halo(gcopies, (ks, kr), gout.at[pair, HT], gout.at[pair, 0], 1, 0, 1)
    halo(gcopies, (ks, kr), gout.at[pair, 1], gout.at[pair, HT + 1], 2, 0, 15)
    halo(gcopies, (ks, kr), gout.at[pair, HT], gout.at[pl.ds(2, 2), 0], 3, 7, 1)
    halo(gcopies, (ks, kr), gout.at[pair, 1], gout.at[pl.ds(2, 2), HT + 1], 4, 7, 15)

    def turn(f, _):
        for half in range(2):
            cells = ext[f, pl.ds(3 * half, 3)].reshape(3 * WD, CH)
            extt[:, pl.ds(pl.multiple_of(f * 6 * WD + half * 3 * WD, WD), 3 * WD)] = cells.T
        return 0

    lax.fori_loop(0, 4, turn, 0)
    gw[:, TAPROWS:, :] = jnp.zeros((3, 16, 128), F32)

    core_copies = []

    def core_send(k):
        def one(r, _):
            at = ((2 * k + 1 - core) * 16 + r) * OWN
            for p in range(3):
                cs[(k * 16 + r) * 3 + p] = gw[p, pl.ds(at, PAD)].astype(BF)
            return 0

        lax.fori_loop(0, 16, one, 0)
        core_copies.append(send(cs.at[pl.ds(48 * k, 48)], cr.at[pl.ds(48 * k, 48)], css.at[k], crs.at[k], twin))

    for a in range(3):
        left = jnp.concatenate(
            [
                jnp.concatenate(
                    [extt[:, ((f + a) * 6 + b) * WD : ((f + a) * 6 + b) * WD + FLAT] for f in range(FR)], axis=1
                )
                for b in range(3)
            ],
            axis=0,
        )
        part = jnp.dot(left, gsh[...], preferred_element_type=F32)
        for b in range(3):
            for c in range(3):
                at = (9 * a + 3 * b + c) * CH
                for p in range(3):
                    lane = c * CH + p * 128
                    gw[p, at : at + CH, :] = part[b * CH : b * CH + CH, lane : lane + 128]
        for k in ((0,), (1,), (2, 3))[a]:
            core_send(k)

    def total(p, q):
        coords = [None, None, None]
        for axis, at in zip(ORDERS[p], q):
            coords[axis] = pick(axis, at)
        lane = coords[1] * 4 + coords[2]
        start = ((2 * coords[0] + core) * 16 + lane) * OWN
        return gw[p, pl.ds(start, PAD)] + cr[(coords[0] * 16 + lane) * 3 + p].astype(F32)

    for copy in core_copies:
        copy.wait()

    def step1(i, _):
        for p in range(3):
            cs[32 * p + i] = total(p, (2 + i // 16, (i // 4) % 4, i % 4)).astype(BF)
        return 0

    lax.fori_loop(0, 32, step1, 0)
    step1_copies = [
        send(cs.at[pl.ds(32 * p, 32)], r1.at[p], ss.at[p], rs.at[p], peer(ORDERS[p][0], 2)) for p in range(3)
    ]

    for copy in gcopies:
        copy.wait()

    @pl.when(tm == 7)
    def _():
        gout[2:4] = jnp.zeros((2, HT + 2, WD, CH), BF)

    @pl.when(row == 0)
    def _():
        gout[:, 0] = jnp.zeros((4, WD, CH), BF)

    @pl.when(row == 15)
    def _():
        gout[:, HT + 1] = jnp.zeros((4, WD, CH), BF)

    gacc[...] = jnp.zeros_like(gacc)

    def backward(f):
        left = jnp.concatenate(
            [gout[f + 2 - t // 3, pl.ds(2 - t % 3, HT)].reshape(FLAT, CH) for t in range(9)], axis=1
        )
        right = jnp.concatenate([wgt[3 * t : 3 * t + 3].reshape(3 * CH, CH) for t in range(9)], axis=1)
        prod[...] = lax.dot_general(left, right, (((1,), (1,)), ((), ())), preferred_element_type=F32)

        def one_row(r, _):
            at = pl.ds(pl.multiple_of(r * WD, WD), WD)
            grad_soft = up(prod[at, 0:CH]) + prod[at, CH : 2 * CH] + down(prod[at, 2 * CH : 3 * CH])
            _, inverse, normed = normalise(lat[f, r])
            grad_act = grad_soft * slope(normed * g_row)
            per_cell = grad_act * normed
            gacc[...] += jnp.sum(per_cell.reshape(WD // 8, 8, CH), axis=0)
            scaled = grad_act * g_row
            mean = jnp.mean(per_cell * g_row, axis=-1, keepdims=True)
            out_lat[f, r] = (gout[f, 1 + r].astype(F32) + inverse * (scaled - normed * mean)).astype(BF)
            return 0

        lax.fori_loop(0, HT, one_row, 0)

    backward(0)

    for copy in step1_copies:
        copy.wait_recv()

    def step2(i, _):
        for p in range(3):
            value = total(p, (1, i // 4, i % 4)) + r1[p, 16 + i].astype(F32)
            cs[96 + 16 * p + i] = value.astype(BF)
        return 0

    lax.fori_loop(0, 16, step2, 0)
    step2_copies = [
        send(cs.at[pl.ds(96 + 16 * p, 16)], r2.at[p], ss.at[3 + p], rs.at[3 + p], peer(ORDERS[p][0], 1)) for p in range(3)
    ]

    backward(1)

    gain_copies = []
    gt[tm] = gacc[...]
    for d in range(1, 8):
        gain_copies.append(
            send(gacc, gt.at[tm], gss.at[d - 1], grs.at[d - 1], {"tm": (tm + d) % 8, "rows": row})
        )

    for copy in step2_copies:
        copy.wait_recv()

    def step3(i, _):
        q2, q3 = 1 + i // 4, i % 4
        at = q2 * 4 + q3
        for p in range(3):
            value = total(p, (0, q2, q3)) + r1[p, at].astype(F32) + r2[p, at].astype(F32)
            cs[144 + 12 * p + i] = value.astype(BF)
        return 0

    lax.fori_loop(0, 12, step3, 0)
    step3_copies = []
    for p in range(3):
        for q in (1, 2, 3):
            n = 6 + 3 * p + q - 1
            part = pl.ds(4 * (q - 1), 4)
            step3_copies.append(
                send(cs.at[pl.ds(144 + 12 * p + 4 * (q - 1), 4)], r3.at[p, part], ss.at[n], rs.at[n], peer(ORDERS[p][1], q))
            )

    for copy in gain_copies:
        copy.wait()
    gsum = gt[0]
    for d in range(1, 8):
        gsum = gsum + gt[d]
    gmid[0] = gsum
    gx[place[1]] = gsum
    xcopies = [
        send(gmid.at[0], gx.at[place[1]], gss.at[6 + q], grs.at[6 + q], peer(1, q)) for q in (1, 2, 3)
    ]

    for copy in step3_copies:
        copy.wait_recv()

    def step4(i, _):
        q3 = 1 + i
        for p in range(3):
            value = total(p, (0, 0, q3)) + r1[p, q3].astype(F32) + r2[p, q3].astype(F32)
            for q in range(3):
                value = value + r3[p, 4 * q + q3].astype(F32)
            cs[180 + 3 * p + i] = value.astype(BF)
        return 0

    lax.fori_loop(0, 3, step4, 0)
    step4_copies = []
    for p in range(3):
        for q in (1, 2, 3):
            n = 15 + 3 * p + q - 1
            step4_copies.append(
                send(cs.at[180 + 3 * p + q - 1], r4.at[p, q - 1], ss.at[n], rs.at[n], peer(ORDERS[p][2], q))
            )

    for copy in xcopies:
        copy.wait()
    gsum = gx[0] + gx[1] + gx[2] + gx[3]
    gmid[1] = gsum
    gz[place[2]] = gsum
    zcopies = [
        send(gmid.at[1], gz.at[place[2]], gss.at[9 + q], grs.at[9 + q], peer(2, q)) for q in (1, 2, 3)
    ]

    for copy in step4_copies:
        copy.wait_recv()
    for p in range(3):
        value = total(p, (0, 0, 0)) + r1[p, 0].astype(F32) + r2[p, 0].astype(F32)
        for q in range(3):
            value = value + r3[p, 4 * q].astype(F32)
        for q in range(3):
            value = value + r4[p, q].astype(F32)
        out_w[:, p * 128 : p * 128 + 128] = value[:OWN]

    for copy in zcopies:
        copy.wait()
    gsum = gz[0] + gz[1] + gz[2] + gz[3]
    out_gain[...] = jnp.sum(gsum, axis=0, keepdims=True)

    for copy in copies + step1_copies + step2_copies + step3_copies + step4_copies:
        copy.wait_send()


def shards(latents, reward_weight, norm_gain, conv_weight, scored_frames):
    vm = pl.BlockSpec(memory_space=pltpu.VMEM)
    dma = pltpu.SemaphoreType.DMA
    blocks = lambda *lead: pltpu.VMEM(lead + (PAD, 128), BF)
    lat, wsum, gsum = pl.pallas_call(
        kernel,
        out_shape=(
            jax.ShapeDtypeStruct((FR, HT, WD, CH), BF),
            jax.ShapeDtypeStruct((OWN, CH), F32),
            jax.ShapeDtypeStruct((1, CH), F32),
        ),
        in_specs=[vm, vm, vm, pl.BlockSpec(memory_space=pl.ANY), pl.BlockSpec(memory_space=pltpu.SMEM)],
        out_specs=(vm, vm, vm),
        scratch_shapes=[
            pltpu.VMEM((27, CH, CH), BF),
            pltpu.VMEM((4, HT + 2, WD, CH), BF),
            pltpu.VMEM((CH, 4 * (HT + 2) * WD), BF),
            pltpu.VMEM((4, HT + 2, WD, CH), BF),
            pltpu.VMEM((FR * FLAT, 3 * CH), BF),
            pltpu.VMEM((FLAT, 3 * CH), F32),
            pltpu.VMEM((3, TAPROWS + 16, 128), F32),
            blocks(192),
            blocks(192),
            blocks(3, 32),
            blocks(3, 16),
            blocks(3, 12),
            blocks(3, 3),
            pltpu.VMEM((8, CH), F32),
            pltpu.VMEM((8, 8, CH), F32),
            pltpu.VMEM((4, 8, CH), F32),
            pltpu.VMEM((4, 8, CH), F32),
            pltpu.VMEM((2, 8, CH), F32),
            dma,
            dma((5,)),
            dma((5,)),
            dma((5,)),
            dma((5,)),
            dma((4,)),
            dma((4,)),
            dma((24,)),
            dma((24,)),
            dma((13,)),
            dma((13,)),
        ],
        compiler_params=pltpu.CompilerParams(
            collective_id=0, has_side_effects=True, vmem_limit_bytes=61 * 1024 * 1024
        ),
        cost_estimate=pl.CostEstimate(flops=24_500_000_000, bytes_accessed=12_000_000, transcendentals=1_500_000),
    )(latents, reward_weight, norm_gain.reshape(1, CH), conv_weight, scored_frames)
    return lat, wsum, gsum.reshape(CH)


def solution(mesh):
    placed = (P("tm", "rows", None, None), P("tm", "rows", None, None), P(), P(), P())
    return jax.shard_map(
        shards,
        mesh=mesh,
        in_specs=placed,
        out_specs=(P("tm", "rows", None, None), P(("tm", "rows"), None), P()),
        check_vma=False,
    )
```

time: 960 us -> 95.6 us (0.10)
  blocking collectives: 457 us -> 0 us
  matrix products: 223 us -> 0 us
  local copies, waits for them, and re-layouts: 166 us -> 4.91 us
  Pallas kernels: 0 us -> 88.5 us
  starting transfers between devices: 74.3 us -> 0 us
  other arithmetic: 20 us -> 1.27 us
  waiting for transfers between devices: 9.67 us -> 0 us
    unnamed x1 -> x0, blocking collectives: 393 us -> none
    dot_general x81 -> x0, matrix products: 223 us -> none  [the longest x27 94.2 us: shards(): jnp.dot(window, conv_weight[offset], preferred_element_type=jnp.float32)]
    slice x55 -> x0, local copies, waits for them, and re-layouts: 119 us -> none  [the longest x27 63.8 us: shards(): soft_pad[frame_off:frame_off + frames, row_off:row_off + height, col_off:...]
    pallas_call x0 -> x1, Pallas kernels: none -> 88.5 us  [shards(): pl.pallas_call(kernel, out_shape=(jax.ShapeDtypeStruct((FR, HT, WD, CH),...]
    psum x1 -> x0, blocking collectives: 63.9 us -> none  [shards(): lax.psum(jnp.sum(grad_act * normed, axis=(0, 1, 2)), ('tm', 'rows'))]
    unnamed x20 -> x0, starting transfers between devices: 62.9 us -> none
    unnamed x52 -> x2, local copies, waits for them, and re-layouts: 40.3 us -> 3.66 us
    ppermute x6 -> x0, starting transfers between devices: 11.4 us -> none  [the longest x2 5.68 us: extended(): lax.ppermute(tail, axis, [(i, (i + 1) % count) for i in range(ends)])]
  transfers between devices with their start and end apart: 26 -> 0, of which waited for: 3 -> 0; matrix products, arithmetic and copies ran while one was open for 6% -> 0% of each run, Pallas kernels for 0% -> 0%
where the time goes in v1:
time: 95.6 us; the launch traced here: 95.4 us
  Pallas kernels  88.5 us (93%)
  local copies, waits for them, and re-layouts  4.91 us (5%)
  other arithmetic  1.27 us (1%)
    pallas_call x1, Pallas kernels, shards(): pl.pallas_call(kernel, out_shape=(jax.ShapeDtypeStruct((FR, HT, WD, CH),...  88.5 us
    unnamed x2, local copies, waits for them, and re-layouts  3.66 us

profile of v1, /device:TPU:0, one launch (start us, length us, event | category | flops | bytes accessed | tf_op | source)
XLA Modules:
  0.0 95.4 jit_solution(10336534467913958851)
XLA Ops:
  0.6 1.2 %reshape.12.gain = f32[1,384]{1,0:T(1,128)} reshape(f32[384]{0:T(512)} %param.7) | data formatting | bytes 3072 | tf_op jit(solution)/shard_map/reshape | solution.py:460
  1.9 88.5 %shard_map.76 = (bf16[2,4,128,384]{3,2,1,0:T(8,128)(2,1)}, f32[81,384]{1,0:T(8,128)}, f32[1,384]{1,0:T(1,128)}) custom-call(bf16[2,4,128,384]{3,2,1,0:T(8,128)(2,1)} %lat.1, bf16[2,4,128,384]{3,2,1,0:T(8,128)(2,1)} %rew.1, f32[1,384]{1,0:T(1,128)} %reshape.12.gain, bf16[27,384,384]{2,1,0:T(8,128)(2,1)} %wgt_hbm.1, s32[8]{0:T(128)} %scored.1), custom_call_target="tpu_custom_call" | custom-call | flops 24500000768 | bytes 12000000 | tf_op jit(solution)/shard_map/pallas_call | solution.py:416
  90.4 1.3 %reduce = f32[384]{0:T(512)} reduce(f32[1,384]{1,0:T(1,128)} %get-tuple-element.8, f32[]{:T(128)} %constant.2), dimensions={0}, to_apply=%get-tuple-element.8.reduce_sub_computation | reduce | bytes 3076 | tf_op jit(solution)/shard_map/pallas_call | solution.py:416
  91.7 2.1 %copy.10 = bf16[2,4,128,384]{3,2,1,0:T(8,128)(2,1)} copy(bf16[2,4,128,384]{3,2,1,0:T(8,128)(2,1)} %get-tuple-element.12) | data formatting | bytes 1572864
  93.8 1.6 %copy.11 = f32[81,384]{1,0:T(8,128)} copy(f32[81,384]{1,0:T(8,128)} %get-tuple-element.13) | data formatting | bytes 248832

commit v2 on v1

v2 whole, which is shorter than its diff:
```python
import functools

import jax
import jax.numpy as jnp
from jax import lax
from jax.experimental import pallas as pl
from jax.experimental.pallas import tpu as pltpu
from jax.sharding import PartitionSpec as P

MESH = pl.DeviceIdType.MESH
EPSILON = 1e-06
BF = jnp.bfloat16
F32 = jnp.float32
FR, HT, WD, CH = 2, 4, 128, 384
FLAT = HT * WD
OWN = 81
PAD = 96
SUB = 32
SLAB = 16 * OWN
TAPROWS = 27 * CH
ORDERS = ((0, 1, 2), (1, 2, 0), (2, 0, 1))
CHUNKS = ((0, 1), (2,))


def sigmoid(value):
    return 0.5 + 0.5 * jnp.tanh(0.5 * value)


def slope(value):
    s = sigmoid(value)
    return s * (1.0 + value * (1.0 - s))


def normalise(cells):
    wide = cells.astype(F32)
    inverse = lax.rsqrt(jnp.mean(wide * wide, axis=-1, keepdims=True) + EPSILON)
    return wide, inverse, wide * inverse


def down(x):
    row = lax.broadcasted_iota(jnp.int32, x.shape, 0)
    return jnp.where(row == 0, 0.0, pltpu.roll(x, 1, 0))


def up(x):
    row = lax.broadcasted_iota(jnp.int32, x.shape, 0)
    return jnp.where(row == x.shape[0] - 1, 0.0, pltpu.roll(x, x.shape[0] - 1, 0))


def kernel(
    lat_hbm, rew_hbm, gain, wgt_hbm, scored,
    out_lat, out_w, out_gain,
    lat, rew, res, wgt, ext, extt, gout, gsh, prod, gw,
    cs, cr, r1, r2, r3, r4, fin,
    gacc, gt, gx, gz, gmid,
    wsem, osem, hs, hr, ks, kr, css, crs, ss, rs, gss, grs,
):
    tm = lax.axis_index("tm")
    row = lax.axis_index("rows")
    core = tm % 2
    place = (tm // 2, row // 4, row % 4)

    def device(coords, c):
        return {"tm": coords[0] * 2 + c, "rows": coords[1] * 4 + coords[2]}

    def flip(v):
        return v + 1 - 2 * (v % 2)

    other = []
    for v in place:
        second = core * flip(v) + (1 - core) * (3 - v)
        first = core * (3 - v) + (1 - core) * flip(v)
        other.append((v, second, first, (v + 2) % 4))

    def peer(axis, q):
        coords = list(place)
        coords[axis] = other[axis][q]
        return device(coords, core)

    def pick(axis, q):
        if isinstance(q, int):
            return other[axis][q]
        o = other[axis]
        return jnp.where(q == 0, o[0], jnp.where(q == 1, o[1], jnp.where(q == 2, o[2], o[3])))

    row_next, row_prev = (row + 1) % 16, (row + 15) % 16
    twin = {"tm": tm + 1 - 2 * core, "rows": row}

    barrier = pltpu.get_barrier_semaphore()
    partners = [{"tm": tm, "rows": row_next}, {"tm": tm, "rows": row_prev}]
    partners += [{"tm": (tm + d) % 8, "rows": row} for d in range(1, 8)]
    partners += [peer(axis, q) for axis in (1, 2) for q in (1, 2, 3)]
    for partner in partners:
        pl.semaphore_signal(barrier, 1, device_id=partner, device_id_type=MESH)

    load_lat = pltpu.make_async_copy(lat_hbm, lat, wsem.at[0])
    load = pltpu.make_async_copy(wgt_hbm, wgt, wsem.at[1])
    load_rew = pltpu.make_async_copy(rew_hbm, rew, wsem.at[2])
    load_lat.start()
    load.start()
    load_rew.start()

    g_row = gain[...].reshape(1, CH)
    zero_block = jnp.zeros((2, WD, CH), BF)

    def own_soft(i, _):
        f, r = i // HT, i % HT
        _, _, normed = normalise(lat[f, r])
        act = normed * g_row
        ext[2 + f, 1 + r] = (act * sigmoid(act)).astype(BF)
        return 0

    load_lat.wait()
    lax.fori_loop(0, FR * HT, own_soft, 0)

    def product(f, taps):
        left = jnp.concatenate(
            [ext[f + a, b : b + HT].reshape(FLAT, CH) for a, b in taps], axis=1
        )
        right = jnp.concatenate(
            [jnp.concatenate([wgt[9 * a + 3 * b + c] for c in range(3)], axis=1) for a, b in taps], axis=0
        )
        return jnp.dot(left, right, preferred_element_type=F32)

    load.wait()
    prod[0] = product(0, [(2, 1)])
    prod[1] = product(1, [(1, 1), (2, 1)])

    pl.semaphore_wait(barrier, len(partners))

    def copy_of(src, dst, a, b, target):
        return pltpu.make_async_remote_copy(
            src_ref=src, dst_ref=dst, send_sem=a, recv_sem=b, device_id=target, device_id_type=MESH
        )

    def send(*args):
        copy = copy_of(*args)
        copy.start()
        return copy

    class Halo:
        def __init__(self, ref, own, far, step, order, sems):
            self.own, self.far, self.ref, self.order = own, far, ref, order
            self.giver = core == (0 if step == 1 else 1)
            self.end = 0 if step == 1 else 7
            up_row, down_row = {"tm": tm, "rows": row_next}, {"tm": tm, "rows": row_prev}
            slab = {"tm": (tm + step) % 8, "rows": row}
            mine = pl.ds(own, 2)
            theirs = pl.ds(far, 2)

            def make(i, src, dst, target):
                return copy_of(src, dst, sems[0].at[i], sems[1].at[i], target)

            self.rows = [
                make(0, ref.at[mine, HT], ref.at[mine, 0], up_row),
                make(1, ref.at[mine, 1], ref.at[mine, HT + 1], down_row),
            ]
            self.edges, self.inner, self.relay = {}, {}, {}
            for k in order:
                self.edges[k] = [
                    make(2 + 2 * k, ref.at[own + k, HT], ref.at[far + k, HT], slab),
                    make(3 + 2 * k, ref.at[own + k, 1], ref.at[far + k, 1], slab),
                ]
                inside = pl.ds(2, HT - 2)
                self.inner[k] = [make(6 + k, ref.at[own + k, inside], ref.at[far + k, inside], slab)]
                self.relay[k] = [
                    make(10 + 2 * k, ref.at[far + k, HT], ref.at[far + k, 0], up_row),
                    make(11 + 2 * k, ref.at[far + k, 1], ref.at[far + k, HT + 1], down_row),
                ]
            self.forward = [
                make(8, ref.at[mine, 0], ref.at[theirs, 0], twin),
                make(9, ref.at[mine, HT + 1], ref.at[theirs, HT + 1], twin),
            ]

        def begin(self):
            for copy in self.rows:
                copy.start()
            for k in self.order:
                for copy in self.edges[k]:
                    copy.start()
            for k in self.order:
                for copy in self.inner[k]:
                    copy.start()

        def take_rows(self):
            for copy in self.rows:
                copy.wait_recv()
            self.clear(self.own, 2)

            @pl.when(self.giver)
            def _():
                for copy in self.forward:
                    copy.start()

        def take_edges(self, k):
            for copy in self.edges[k]:
                copy.wait_recv()

            @pl.when(self.giver)
            def _():
                for copy in self.relay[k]:
                    copy.start()

        def take_rest(self, k):
            for copy in self.inner[k]:
                copy.wait_recv()

            @pl.when(self.giver)
            def _():
                for copy in self.relay[k]:
                    copy.wait()

            if k == self.order[0]:

                @pl.when(jnp.logical_not(self.giver))
                def _():
                    for copy in self.forward:
                        copy.wait_recv()

            self.clear(self.far + k, 1)

            @pl.when(tm == self.end)
            def _():
                self.ref[self.far + k] = jnp.zeros((HT + 2, WD, CH), BF)

        def clear(self, frame, count):
            @pl.when(row == 0)
            def _():
                self.ref[frame : frame + count, 0] = zero_block[:count]

            @pl.when(row == 15)
            def _():
                self.ref[frame : frame + count, HT + 1] = zero_block[:count]

        def finish(self):
            @pl.when(self.giver)
            def _():
                for copy in self.forward:
                    copy.wait_send()

            for copy in self.rows:
                copy.wait_send()
            for k in self.order:
                for copy in self.edges[k] + self.inner[k]:
                    copy.wait_send()

    soft_halo = Halo(ext, 2, 0, 1, (1, 0), (hs, hr))
    soft_halo.begin()

    def turn(f, rows):
        for r in rows:
            extt[:, (f * 6 + r) * WD : (f * 6 + r + 1) * WD] = ext[f, r].T

    def emit(f):
        frame = tm * FR + f
        mask = jnp.float32(0.0)
        for i in range(8):
            mask = jnp.maximum(mask, jnp.where(scored[i] == frame, 1.0, 0.0))

        def one_row(r, _):
            at = pl.ds(pl.multiple_of(r * WD, WD), WD)
            conv = down(prod[f, at, 0:CH]) + prod[f, at, CH : 2 * CH] + up(prod[f, at, 2 * CH : 3 * CH])
            value = lat[f, r].astype(F32) + conv
            grad = mask * rew[f, r].astype(F32) * slope(value)
            low = grad.astype(BF)
            wide = low.astype(F32)
            gout[f, 1 + r] = low
            to = pl.ds(pl.multiple_of(f * FLAT + r * WD, WD), WD)
            for c, shifted in enumerate((up(wide).astype(BF), low, down(wide).astype(BF))):
                gsh[to, c * 256 : c * 256 + 256] = shifted[:, :256]
                gsh[to, 768 + c * 128 : 896 + c * 128] = shifted[:, 256:]
            return 0

        lax.fori_loop(0, HT, one_row, 0)

    for f in (2, 3):
        turn(f, (1, 2, 3, 4))
    soft_halo.take_rows()
    prod[0] += product(0, [(2, 0), (2, 2)])
    soft_halo.take_edges(1)
    prod[1] += product(1, [(1, 0), (1, 2), (2, 0), (2, 2)])
    load_rew.wait()
    for f in (2, 3):
        turn(f, (0, 5))
    soft_halo.take_edges(0)
    soft_halo.take_rest(1)
    prod[1] += product(1, [(0, 0), (0, 1), (0, 2)])
    emit(1)
    prod[0] += product(0, [(1, 0), (1, 1), (1, 2)])
    turn(1, range(6))
    soft_halo.take_rest(0)
    prod[0] += product(0, [(0, 0), (0, 1), (0, 2)])
    emit(0)

    grad_halo = Halo(gout, 0, 2, -1, (0, 1), (ks, kr))
    grad_halo.begin()

    turn(0, range(6))
    gw[:, TAPROWS:, :] = jnp.zeros((3, 16, 128), F32)

    def start_of(block):
        return pl.multiple_of(block * OWN // 16 * 16, 16)

    def unit(n, count=1):
        return pl.ds(pl.multiple_of(SUB * n, SUB), SUB * count)

    class Chunk:
        def __init__(self, n):
            self.parts = CHUNKS[n]
            self.width = len(self.parts)
            self.base = 3 * sum(len(c) for c in CHUNKS[:n])
            self.sem = 24 * n
            self.csem = 3 * n
            self.core_copies = []
            self.copies = {}

        def area(self, blocks):
            return self.base * blocks

        def core_send(self, n, low, high):
            lead = self.base * 64 * SUB
            for k in range(low, high):
                for pi, p in enumerate(self.parts):
                    at = lead + (k * self.width + pi) * SLAB

                    def one(i, _):
                        step = SLAB // 9
                        src = pl.multiple_of((2 * k + 1 - core) * SLAB + i * step, 16)
                        dst = pl.multiple_of(at + i * step, 16)
                        cs[pl.ds(dst, step)] = gw[p, pl.ds(src, step)].astype(BF)
                        return 0

                    lax.fori_loop(0, 9, one, 0)
            rows = self.width * (high - low) * SLAB
            src = pl.ds(lead + low * self.width * SLAB, rows)
            dst = pl.ds(self.base // 3 * 4 * SLAB + low * self.width * SLAB, rows)
            self.core_copies.append(
                send(cs.at[src], cr.at[dst], css.at[self.csem + n], crs.at[self.csem + n], twin)
            )

        def core_done(self):
            for copy in self.core_copies:
                copy.wait()

        def total(self, pi, j, q):
            coords = [None, None, None]
            for axis, at in zip(ORDERS[j], q):
                coords[axis] = pick(axis, at)
            lane = coords[1] * 4 + coords[2]
            start = start_of((2 * coords[0] + core) * 16 + lane)
            held = gw[self.parts[pi], pl.ds(pl.multiple_of(start + SUB * j, 16), SUB)]
            near = start - (2 * coords[0] + core) * SLAB + SUB * j
            at = (self.base // 3 * 4 + coords[0] * self.width + pi) * SLAB + near
            return held + cr[pl.ds(pl.multiple_of(at, 16), SUB)].astype(F32)

        def got(self, ref, blocks, j, i, pi):
            return ref[unit(self.area(blocks) + (j * blocks + i) * self.width + pi)].astype(F32)

        def value(self, step, pi, j, q):
            value = self.total(pi, j, q)
            if step >= 2:
                value = value + self.got(r1, 32, j, (q[0] * 4 + q[1]) * 4 + q[2], pi)
            if step >= 3:
                value = value + self.got(r2, 16, j, q[1] * 4 + q[2], pi)
            if step >= 4:
                for n in range(3):
                    value = value + self.got(r3, 12, j, 4 * n + q[2], pi)
            if step >= 5:
                for n in range(3):
                    value = value + self.got(r4, 3, j, n, pi)
            return value

        def step(self, step):
            if step > 1:
                for copy in self.copies[step - 1]:
                    copy.wait_recv()
            first = (None, 0, 96, 144, 180)[step]
            blocks = (None, 32, 16, 12, 3)[step]
            into = (None, r1, r2, r3, r4)[step]
            place_of = (
                None,
                lambda i: (2 + i // 16, i // 4 % 4, i % 4),
                lambda i: (1, i // 4, i % 4),
                lambda i: (0, 1 + i // 4, i % 4),
                lambda i: (0, 0, 1 + i),
            )[step]
            lead = self.area(64) + first * self.width

            def one(i, _):
                for j in range(3):
                    for pi in range(self.width):
                        value = self.value(step, pi, j, place_of(i)).astype(BF)
                        cs[unit(lead + (j * blocks + i) * self.width + pi)] = value
                return 0

            lax.fori_loop(0, blocks, one, 0)
            out = []
            for j in range(3):
                axis = ORDERS[j][(None, 0, 0, 1, 2)[step]]
                for n, q in enumerate(((2,), (1,), (1, 2, 3), (1, 2, 3))[step - 1]):
                    span = blocks // (1 if step < 3 else 3) * self.width
                    at = j * blocks * self.width + n * span
                    sem = self.sem + (None, j, 3 + j, 6 + 3 * j + n, 15 + 3 * j + n)[step]
                    out.append(
                        send(
                            cs.at[unit(lead + at, span)],
                            into.at[unit(self.area(blocks) + at, span)],
                            ss.at[sem],
                            rs.at[sem],
                            peer(axis, q),
                        )
                    )
            self.copies[step] = out

        def last(self):
            for copy in self.copies[4]:
                copy.wait_recv()
            for pi, p in enumerate(self.parts):
                for j in range(3):
                    fin[p, SUB * j : SUB * j + SUB] = self.value(5, pi, j, (0, 0, 0))
            offset = (tm * 16 + row) * OWN % 16
            for p in self.parts:
                out_w[:, p * 128 : p * 128 + 128] = fin[p, pl.ds(offset, OWN)]

        def finish(self):
            for copies in self.copies.values():
                for copy in copies:
                    copy.wait_send()

    def outer(n, a):
        parts = CHUNKS[n]
        wide = 128 * len(parts)
        left = jnp.concatenate(
            [
                jnp.concatenate(
                    [extt[:, ((f + a) * 6 + b) * WD : ((f + a) * 6 + b) * WD + FLAT] for f in range(FR)], axis=1
                )
                for b in range(3)
            ],
            axis=0,
        )
        lanes = slice(384 * parts[0], 384 * parts[0] + 3 * wide)
        part = jnp.dot(left, gsh[:, lanes], preferred_element_type=F32)
        for b in range(3):
            for c in range(3):
                at = (9 * a + 3 * b + c) * CH
                for pi, p in enumerate(parts):
                    lane = c * wide + pi * 128
                    gw[p, at : at + CH, :] = part[b * CH : b * CH + CH, lane : lane + 128]

    one, two = Chunk(0), Chunk(1)
    outer(0, 0)
    one.core_send(0, 0, 1)
    outer(0, 1)
    one.core_send(1, 1, 2)
    grad_halo.take_rows()
    outer(0, 2)
    one.core_send(2, 2, 4)
    grad_halo.take_edges(0)
    outer(1, 0)
    grad_halo.take_edges(1)
    outer(1, 1)
    one.core_done()
    one.step(1)
    outer(1, 2)
    two.core_send(0, 0, 4)
    grad_halo.take_rest(0)
    two.core_done()
    two.step(1)
    grad_halo.take_rest(1)

    gacc[...] = jnp.zeros_like(gacc)
    stores = []

    def backward(f, half):
        left = jnp.concatenate(
            [
                gout[f + 2 - t // 3, 2 * half + 2 - t % 3 : 2 * half + 4 - t % 3].reshape(2 * WD, CH)
                for t in range(9)
            ],
            axis=1,
        )
        right = jnp.concatenate([wgt[3 * t : 3 * t + 3].reshape(3 * CH, CH) for t in range(9)], axis=1)
        prod[f, 0 : 2 * WD] = lax.dot_general(left, right, (((1,), (1,)), ((), ())), preferred_element_type=F32)

        def one_row(i, _):
            r = 2 * half + i
            at = pl.ds(pl.multiple_of(i * WD, WD), WD)
            grad_soft = up(prod[f, at, 0:CH]) + prod[f, at, CH : 2 * CH] + down(prod[f, at, 2 * CH : 3 * CH])
            _, inverse, normed = normalise(lat[f, r])
            grad_act = grad_soft * slope(normed * g_row)
            per_cell = grad_act * normed
            gacc[...] += jnp.sum(per_cell.reshape(WD // 8, 8, CH), axis=0)
            scaled = grad_act * g_row
            mean = jnp.mean(per_cell * g_row, axis=-1, keepdims=True)
            res[f, r] = (gout[f, 1 + r].astype(F32) + inverse * (scaled - normed * mean)).astype(BF)
            return 0

        lax.fori_loop(0, 2, one_row, 0)
        pair = pl.ds(2 * half, 2)
        store = pltpu.make_async_copy(res.at[f, pair], out_lat.at[f, pair], osem.at[2 * f + half])
        store.start()
        stores.append(store)

    backward(0, 0)
    one.step(2)
    backward(0, 1)
    two.step(2)
    backward(1, 0)
    one.step(3)
    backward(1, 1)

    gt[tm] = gacc[...]
    gain_copies = [
        send(gacc, gt.at[tm], gss.at[d - 1], grs.at[d - 1], {"tm": (tm + d) % 8, "rows": row}) for d in range(1, 8)
    ]

    two.step(3)

    for copy in gain_copies:
        copy.wait()
    gsum = gt[0]
    for d in range(1, 8):
        gsum = gsum + gt[d]
    gmid[0] = gsum
    gx[place[1]] = gsum
    xcopies = [
        send(gmid.at[0], gx.at[place[1]], gss.at[6 + q], grs.at[6 + q], peer(1, q)) for q in (1, 2, 3)
    ]

    one.step(4)

    for copy in xcopies:
        copy.wait()
    gsum = gx[0] + gx[1] + gx[2] + gx[3]
    gmid[1] = gsum
    gz[place[2]] = gsum
    zcopies = [
        send(gmid.at[1], gz.at[place[2]], gss.at[9 + q], grs.at[9 + q], peer(2, q)) for q in (1, 2, 3)
    ]

    two.step(4)
    for copy in zcopies:
        copy.wait()
    gsum = gz[0] + gz[1] + gz[2] + gz[3]
    out_gain[...] = jnp.sum(gsum, axis=0)
    for store in stores:
        store.wait()
    soft_halo.finish()
    grad_halo.finish()
    one.last()
    one.finish()
    two.last()
    two.finish()


def hand_on(*refs):
    sems = refs[6]
    copies = [pltpu.make_async_copy(refs[i], refs[3 + i], sems.at[i]) for i in range(3)]
    for copy in copies:
        copy.start()
    for copy in copies:
        copy.wait()


def shards(latents, reward_weight, norm_gain, conv_weight, scored_frames):
    vm = pl.BlockSpec(memory_space=pltpu.VMEM)
    anywhere = pl.BlockSpec(memory_space=pl.ANY)
    dma = pltpu.SemaphoreType.DMA
    units = lambda n: pltpu.VMEM((n * SUB, 128), BF)
    shapes = (
        jax.ShapeDtypeStruct((FR, HT, WD, CH), BF),
        jax.ShapeDtypeStruct((OWN, CH), F32),
        jax.ShapeDtypeStruct((CH,), F32),
    )
    results = pl.pallas_call(
        kernel,
        out_shape=shapes,
        in_specs=[anywhere, anywhere, vm, anywhere, pl.BlockSpec(memory_space=pltpu.SMEM)],
        out_specs=(anywhere, vm, vm),
        scratch_shapes=[
            pltpu.VMEM((FR, HT, WD, CH), BF),
            pltpu.VMEM((FR, HT, WD, CH), BF),
            pltpu.VMEM((FR, HT, WD, CH), BF),
            pltpu.VMEM((27, CH, CH), BF),
            pltpu.VMEM((4, HT + 2, WD, CH), BF),
            pltpu.VMEM((CH, 4 * (HT + 2) * WD), BF),
            pltpu.VMEM((4, HT + 2, WD, CH), BF),
            pltpu.VMEM((FR * FLAT, 3 * CH), BF),
            pltpu.VMEM((FR, FLAT, 3 * CH), F32),
            pltpu.VMEM((3, TAPROWS + 16, 128), F32),
            units(576),
            pltpu.VMEM((12 * SLAB, 128), BF),
            units(288),
            units(144),
            units(108),
            units(27),
            pltpu.VMEM((3, PAD, 128), F32),
            pltpu.VMEM((8, CH), F32),
            pltpu.VMEM((8, 8, CH), F32),
            pltpu.VMEM((4, 8, CH), F32),
            pltpu.VMEM((4, 8, CH), F32),
            pltpu.VMEM((2, 8, CH), F32),
            dma((3,)),
            dma((4,)),
            dma((14,)),
            dma((14,)),
            dma((14,)),
            dma((14,)),
            dma((6,)),
            dma((6,)),
            dma((48,)),
            dma((48,)),
            dma((13,)),
            dma((13,)),
        ],
        compiler_params=pltpu.CompilerParams(
            collective_id=0, has_side_effects=True, vmem_limit_bytes=61 * 1024 * 1024
        ),
        cost_estimate=pl.CostEstimate(flops=24_500_000_000, bytes_accessed=12_000_000, transcendentals=1_500_000),
    )(latents, reward_weight, norm_gain, conv_weight, scored_frames)
    return tuple(
        pl.pallas_call(
            hand_on,
            out_shape=shapes,
            in_specs=[vm] * 3,
            out_specs=(anywhere,) * 3,
            scratch_shapes=[dma((3,))],
        )(*results)
    )


def solution(mesh):
    placed = (P("tm", "rows", None, None), P("tm", "rows", None, None), P(), P(), P())
    return jax.shard_map(
        shards,
        mesh=mesh,
        in_specs=placed,
        out_specs=(P("tm", "rows", None, None), P(("tm", "rows"), None), P()),
        check_vma=False,
    )
```

time: 95.6 us -> 89.4 us (0.935)
  local copies, waits for them, and re-layouts: 4.91 us -> 0 us
  other arithmetic: 1.27 us -> 0 us
    unnamed x2 -> x0, local copies, waits for them, and re-layouts: 3.66 us -> none
    pallas_call x1 -> x0, other arithmetic: 1.27 us -> none  [shards(): pl.pallas_call(kernel, out_shape=(jax.ShapeDtypeStruct((FR, HT, WD, CH),...]
    reshape x1 -> x0, local copies, waits for them, and re-layouts: 1.25 us -> none  [shards(): norm_gain.reshape(1, CH)]
    pallas_call x1 -> x2, Pallas kernels: 88.5 us -> 88.5 us  [the longest x1 86.3 us: shards(): pl.pallas_call(kernel, out_shape=shapes, in_specs=[anywhere, anywhere, vm...]
where the time goes in v2:
time: 89.4 us; the launch traced here: 89.3 us
  Pallas kernels  88.5 us (99%)
    pallas_call x1, Pallas kernels, shards(): pl.pallas_call(kernel, out_shape=shapes, in_specs=[anywhere, anywhere, vm...  86.3 us
    pallas_call x1, Pallas kernels, shards(): pl.pallas_call(hand_on, out_shape=shapes, in_specs=[vm] * 3, out_specs=(a...  2.16 us

profile of v2, /device:TPU:0, one launch (start us, length us, event | category | flops | bytes accessed | tf_op | source)
XLA Modules:
  0.0 89.3 jit_solution(8235810205492237075)
XLA Ops:
  0.6 86.3 %shard_map.76 = (bf16[2,4,128,384]{3,2,1,0:T(8,128)(2,1)}, f32[81,384]{1,0:T(8,128)}, f32[384]{0:T(512)}) custom-call(bf16[2,4,128,384]{3,2,1,0:T(8,128)(2,1)} %lat_hbm.1, bf16[2,4,128,384]{3,2,1,0:T(8,128)(2,1)} %rew_hbm.1, f32[384]{0:T(512)} %gain.1, bf16[27,384,384]{2,1,0:T(8,128)(2,1)} %wgt_hbm.1, s32[8]{0:T(128)} %scored.1), custom_call_target="tpu_custom_call" | custom-call | flops 24500000768 | bytes 12000000 | tf_op jit(solution)/shard_map/pallas_call | solution.py:576
  86.9 2.2 %shard_map.77 = (bf16[2,4,128,384]{3,2,1,0:T(8,128)(2,1)}, f32[81,384]{1,0:T(8,128)}, f32[384]{0:T(512)}) custom-call(bf16[2,4,128,384]{3,2,1,0:T(8,128)(2,1)} %get-tuple-element.6.refs_0_, f32[81,384]{1,0:T(8,128)} %get-tuple-element.7.refs_1_, f32[384]{0:T(512)} %get-tuple-element.8.refs_2_), custom_call_target="tpu_custom_call" | custom-call | tf_op jit(solution)/shard_map/pallas_call | solution.py:623

commit v3 on v2

--- a/solution.py
+++ b/solution.py
@@ -299,7 +299,7 @@
     gw[:, TAPROWS:, :] = jnp.zeros((3, 16, 128), F32)
 
     def start_of(block):
-        return pl.multiple_of(block * OWN // 16 * 16, 16)
+        return ((block * OWN) >> 4) << 4
 
     def unit(n, count=1):
         return pl.ds(pl.multiple_of(SUB * n, SUB), SUB * count)
@@ -342,22 +342,23 @@
             for copy in self.core_copies:
                 copy.wait()
 
-        def total(self, pi, j, q):
+        def rows_of(self, j, q):
             coords = [None, None, None]
             for axis, at in zip(ORDERS[j], q):
                 coords[axis] = pick(axis, at)
-            lane = coords[1] * 4 + coords[2]
-            start = start_of((2 * coords[0] + core) * 16 + lane)
-            held = gw[self.parts[pi], pl.ds(pl.multiple_of(start + SUB * j, 16), SUB)]
-            near = start - (2 * coords[0] + core) * SLAB + SUB * j
-            at = (self.base // 3 * 4 + coords[0] * self.width + pi) * SLAB + near
-            return held + cr[pl.ds(pl.multiple_of(at, 16), SUB)].astype(F32)
+            slab = 2 * coords[0] + core
+            start = start_of(slab * 16 + coords[1] * 4 + coords[2]) + SUB * j
+            return start, (self.base // 3 * 4 + coords[0] * self.width - slab) * SLAB + start
+
+        def total(self, pi, rows):
+            held = gw[self.parts[pi], pl.ds(pl.multiple_of(rows[0], 16), SUB)]
+            return held + cr[pl.ds(pl.multiple_of(rows[1] + pi * SLAB, 16), SUB)].astype(F32)
 
         def got(self, ref, blocks, j, i, pi):
             return ref[unit(self.area(blocks) + (j * blocks + i) * self.width + pi)].astype(F32)
 
-        def value(self, step, pi, j, q):
-            value = self.total(pi, j, q)
+        def value(self, step, pi, j, q, rows):
+            value = self.total(pi, rows)
             if step >= 2:
                 value = value + self.got(r1, 32, j, (q[0] * 4 + q[1]) * 4 + q[2], pi)
             if step >= 3:
@@ -377,23 +378,28 @@
             first = (None, 0, 96, 144, 180)[step]
             blocks = (None, 32, 16, 12, 3)[step]
             into = (None, r1, r2, r3, r4)[step]
-            place_of = (
-                None,
-                lambda i: (2 + i // 16, i // 4 % 4, i % 4),
-                lambda i: (1, i // 4, i % 4),
-                lambda i: (0, 1 + i // 4, i % 4),
-                lambda i: (0, 0, 1 + i),
-            )[step]
             lead = self.area(64) + first * self.width
 
-            def one(i, _):
-                for j in range(3):
-                    for pi in range(self.width):
-                        value = self.value(step, pi, j, place_of(i)).astype(BF)
-                        cs[unit(lead + (j * blocks + i) * self.width + pi)] = value
+            firsts = (None, (2, 3), (1,), (0,), (0,))[step]
+            thirds = (1, 2, 3) if step == 4 else (0, 1, 2, 3)
+            low, high = ((0, 0), (0, 4), (0, 4), (1, 4), (0, 1))[step]
+
+            def one(q2, _):
+                for q1 in firsts:
+                    for q3 in thirds:
+                        i = q3 - 1 if step == 4 else (q1 - firsts[0]) * 16 + (q2 - low) * 4 + q3
+                        for j in range(3):
+                            q = (q1, q2, q3)
+                            rows = self.rows_of(j, q)
+                            for pi in range(self.width):
+                                value = self.value(step, pi, j, q, rows).astype(BF)
+                                cs[unit(lead + (j * blocks + i) * self.width + pi)] = value
                 return 0
 
-            lax.fori_loop(0, blocks, one, 0)
+            if step == 4:
+                one(0, 0)
+            else:
+                lax.fori_loop(low, high, one, 0)
             out = []
             for j in range(3):
                 axis = ORDERS[j][(None, 0, 0, 1, 2)[step]]
@@ -417,7 +423,7 @@
                 copy.wait_recv()
             for pi, p in enumerate(self.parts):
                 for j in range(3):
-                    fin[p, SUB * j : SUB * j + SUB] = self.value(5, pi, j, (0, 0, 0))
+                    fin[p, SUB * j : SUB * j + SUB] = self.value(5, pi, j, (0, 0, 0), self.rows_of(j, (0, 0, 0)))
             offset = (tm * 16 + row) * OWN % 16
             for p in self.parts:
                 out_w[:, p * 128 : p * 128 + 128] = fin[p, pl.ds(offset, OWN)]

time: 89.4 us -> 84.4 us (0.944)
  Pallas kernels: 88.5 us -> 83.5 us
    pallas_call x1, Pallas kernels: 86.3 us -> 81.3 us  [shards(): pl.pallas_call(kernel, out_shape=shapes, in_specs=[anywhere, anywhere, vm...]
where the time goes in v3:
time: 84.4 us; the launch traced here: 84.3 us
  Pallas kernels  83.5 us (99%)
    pallas_call x1, Pallas kernels, shards(): pl.pallas_call(kernel, out_shape=shapes, in_specs=[anywhere, anywhere, vm...  81.3 us
    pallas_call x1, Pallas kernels, shards(): pl.pallas_call(hand_on, out_shape=shapes, in_specs=[vm] * 3, out_specs=(a...  2.16 us

profile of v3, /device:TPU:0, one launch (start us, length us, event | category | flops | bytes accessed | tf_op | source)
XLA Modules:
  0.0 84.3 jit_solution(3847829200681393813)
XLA Ops:
  0.6 81.3 %shard_map.76 = (bf16[2,4,128,384]{3,2,1,0:T(8,128)(2,1)}, f32[81,384]{1,0:T(8,128)}, f32[384]{0:T(512)}) custom-call(bf16[2,4,128,384]{3,2,1,0:T(8,128)(2,1)} %lat_hbm.1, bf16[2,4,128,384]{3,2,1,0:T(8,128)(2,1)} %rew_hbm.1, f32[384]{0:T(512)} %gain.1, bf16[27,384,384]{2,1,0:T(8,128)(2,1)} %wgt_hbm.1, s32[8]{0:T(128)} %scored.1), custom_call_target="tpu_custom_call" | custom-call | flops 24500000768 | bytes 12000000 | tf_op jit(solution)/shard_map/pallas_call | solution.py:582
  82.0 2.2 %shard_map.77 = (bf16[2,4,128,384]{3,2,1,0:T(8,128)(2,1)}, f32[81,384]{1,0:T(8,128)}, f32[384]{0:T(512)}) custom-call(bf16[2,4,128,384]{3,2,1,0:T(8,128)(2,1)} %get-tuple-element.6.refs_0_, f32[81,384]{1,0:T(8,128)} %get-tuple-element.7.refs_1_, f32[384]{0:T(512)} %get-tuple-element.8.refs_2_), custom_call_target="tpu_custom_call" | custom-call | tf_op jit(solution)/shard_map/pallas_call | solution.py:629
